TPU v7x, 128 devices: a whole 4x4x4 slice. The times are simulated.
128 devices in a mesh: gx: 64 (over x_hi, y, z, core), gy: 2 (over x_lo).
Axes of the slice: x: 4 (x_hi: 2, x_lo: 2; x = x_hi * 2 + x_lo), y: 4, z: 4, core: 2. Of those that a mesh axis runs over, the one named last changes fastest.
Arguments:
- raw_samples: bfloat16 [2048, 131072], P('gx', 'gy'), may hold values from -6 to 6
- delays: int32 [2048], P('gx'), may hold values from 0 to 2047
- grid_slot: int32 [2048], replicated, may hold values from 0 to 2047, each once
Outputs:
- intensity: bfloat16 [1024, 4, 16384], P('gx', 'gy')
Inputs may be any that keep to these rules, and one draw needn't show every extreme that they name: `grid_slot`: each feed has its own slot.
All inputs are finite; a program needn't handle non-finite values.
Results may differ from a plain program's by a relative error of at most 0.0068.
Values may be sent and summed in bfloat16 or wider, within the bound.
No kernel may reach another device: no remote copies, remote signals or barrier semaphores. Data moves between devices by JAX's collectives and lax.ppermute only.
A program may use at most 128 MiB of HBM per device.

v0:
```python
import functools
import math

import jax
import jax.numpy as jnp
import ml_dtypes
import numpy as np
from jax import lax
from jax.experimental import pallas as pl
from jax.experimental.pallas import tpu as pltpu
from jax.sharding import PartitionSpec as P

CHAN = 1024
EW = 4
NS = 256
UP = 16
POLS = 2
PTAPS = 4
UTAPS = 4
NFFT = 2048
NSPAD = 512
BEAMS = 1024
FEEDS = 2048

LANES = 128
PEERS = 128
CPD = CHAN // PEERS
PPG = 2 * LANES // CPD
SPANS = CHAN // (2 * LANES)
FLOC = 32
HALF = 16
BOTH = ("gx", "gy")
VMEM = 56 * 1024 * 1024


def taper(tap_count, seg_length):
    total_len = tap_count * seg_length
    places = np.arange(total_len, dtype=np.float64)
    centre = (places - 0.5 * total_len + 0.5) / seg_length
    hann_part = 0.5 - 0.5 * np.cos(2.0 * math.pi * (places + 0.5) / total_len)
    return (np.sinc(centre) * hann_part).reshape(tap_count, seg_length).astype(np.float32)


def dft_table():
    rows = np.arange(NFFT // 2)
    cols = np.arange(CHAN).reshape(SPANS, LANES, 2).transpose(0, 2, 1)
    phases = (rows[None, None, :, None] * cols[:, :, None, :] % NFFT) * (2.0 * math.pi / NFFT)
    norm_scale = 1.0 / math.sqrt(NFFT)
    both = np.concatenate([np.cos(phases), -np.sin(phases)], axis=3) * norm_scale
    return both.astype(np.float32).astype(ml_dtypes.bfloat16)


def row_table():
    place = np.arange(NS)
    phases = (place[:, None] * place[None, :] % NSPAD) * (2.0 * math.pi / NSPAD)
    norm_scale = 1.0 / math.sqrt(BEAMS)
    both = np.concatenate([np.cos(phases), np.sin(phases)], axis=0) * norm_scale
    return both.astype(np.float32).astype(ml_dtypes.bfloat16)


def sub_table():
    fir = taper(UTAPS, UP)
    q = np.arange(UP)
    phases = (q[:, None] * q[None, :] % UP) * (2.0 * math.pi / UP)
    cosine = fir[:, :, None] * np.cos(phases).astype(np.float32)[None]
    sine = fir[:, :, None] * np.sin(phases).astype(np.float32)[None]
    table = np.zeros((UTAPS, 2, UP, 2, CPD // 2, 2, CPD, UP), np.float32)
    for k in range(CPD):
        table[:, 0, :, k % 2, k // 2, 0, k, :] = cosine
        table[:, 0, :, k % 2, k // 2, 1, k, :] = -sine
        table[:, 1, :, k % 2, k // 2, 0, k, :] = sine
        table[:, 1, :, k % 2, k // 2, 1, k, :] = cosine
    table = table.reshape(UTAPS, 2, PPG, CPD // 2, 2 * LANES)
    return np.concatenate([table, table], axis=2).astype(ml_dtypes.bfloat16)


def front_kernel(late, raw_ref, halo_ref, w_ref, tab_ref, cos_ref, sin_ref, base_ref, prev_ref, out_ref, *scratch):
    del prev_ref
    ext_ref, x_ref, t_ref, o_ref, raw_sems, tab_sems, out_sems = scratch
    lead = (PTAPS - 1) * NFFT
    part = 1 if late else 0
    if late:
        copies = [
            pltpu.make_async_copy(
                raw_ref.at[:, pl.ds(HALF * NFFT - lead, HALF * NFFT + lead)], ext_ref, raw_sems.at[0]
            )
        ]
    else:
        copies = [
            pltpu.make_async_copy(halo_ref, ext_ref.at[:, pl.ds(0, lead)], raw_sems.at[0]),
            pltpu.make_async_copy(
                raw_ref.at[:, pl.ds(0, HALF * NFFT)], ext_ref.at[:, pl.ds(lead, HALF * NFFT)], raw_sems.at[1]
            ),
        ]
    tables = [pltpu.make_async_copy(tab_ref.at[s], t_ref.at[s], tab_sems.at[s]) for s in range(SPANS)]
    for copy in copies + tables:
        copy.start()
    for copy in copies:
        copy.wait()

    def tile(step, carry):
        at = pl.multiple_of(step * LANES, LANES)
        half = NFFT // 2
        for h in range(2):
            rows = slice(h * 16, h * 16 + 16)
            totals = []
            for side in range(2):
                weights = [w_ref[p : p + 1, pl.ds(at + side * half, LANES)] for p in range(PTAPS)]
                frames = [
                    ext_ref[rows, pl.ds(pl.multiple_of(at + side * half + m * NFFT, LANES), LANES)].astype(jnp.float32)
                    for m in range(HALF + PTAPS - 1)
                ]
                sums = []
                for m in range(HALF):
                    total = frames[m] * weights[0]
                    for p in range(1, PTAPS):
                        total = total + frames[m + p] * weights[p]
                    sums.append(total)
                totals.append(sums)
            for m in range(HALF):
                place = pl.ds(h * 256 + m * 16, 16)
                x_ref[0, place, pl.ds(at, LANES)] = (totals[0][m] + totals[1][m]).astype(jnp.bfloat16)
                x_ref[1, place, pl.ds(at, LANES)] = (totals[0][m] - totals[1][m]).astype(jnp.bfloat16)
        return carry

    lax.fori_loop(0, NFFT // 2 // LANES, tile, 0)

    block = lax.broadcasted_iota(jnp.int32, (16, LANES), 1) // (LANES // PPG)
    bits = [(block // (1 << t)) % 2 == 1 for t in range(5)]
    outs = []
    for s in range(SPANS):
        tables[s].wait()
        spectra = [jnp.dot(x_ref[odd], t_ref[s, odd], preferred_element_type=jnp.float32) for odd in range(2)]
        for h in range(2):
            rows = slice(h * 16, h * 16 + 16)
            cl, sl = cos_ref[rows, :], sin_ref[rows, :]
            parts = [[None] * PPG, [None] * PPG]
            for odd in range(2):
                at = s * 2 + odd
                ca, sa = base_ref[rows, at : at + 1], base_ref[rows, 8 + at : 9 + at]
                cosine, sine = ca * cl - sa * sl, sa * cl + ca * sl
                for m in range(HALF):
                    i = m * 2 + odd
                    row = h * 256 + m * 16
                    real = spectra[odd][row : row + 16, :LANES]
                    imag = spectra[odd][row : row + 16, LANES:]
                    turned = (real * cosine + imag * sine, imag * cosine - real * sine)
                    for x in range(2):
                        value = pltpu.roll(turned[x], i * (LANES // PPG), 1) if i else turned[x]
                        parts[x][i] = value.astype(jnp.bfloat16)
            for x in range(2):
                held = parts[x]
                for t in range(5):
                    held = [jnp.where(bits[t], held[(i + (1 << t)) % PPG], held[i]) for i in range(PPG)]
                for p in range(PPG):
                    o_ref[s, p, x, rows, :] = held[(PPG - p) % PPG]
        copy = pltpu.make_async_copy(o_ref.at[s], out_ref.at[pl.ds(s * PPG, PPG), part], out_sems.at[s])
        copy.start()
        outs.append(copy)
    for copy in outs:
        copy.wait()


def front(late, raw, halo, weights, table, cosine, sine, base, prev):
    wide = (HALF + PTAPS - 1) * NFFT
    whole = pl.BlockSpec(memory_space=pltpu.VMEM)
    there = pl.BlockSpec(memory_space=pl.ANY)
    return pl.pallas_call(
        functools.partial(front_kernel, late),
        in_specs=[there, there, whole, there, whole, whole, whole, there],
        out_specs=there,
        out_shape=jax.ShapeDtypeStruct((PEERS, 2, 2, FLOC, LANES), jnp.bfloat16),
        scratch_shapes=[
            pltpu.VMEM((FLOC, wide), jnp.bfloat16),
            pltpu.VMEM((2, FLOC * HALF, NFFT // 2), jnp.bfloat16),
            pltpu.VMEM((SPANS, 2, NFFT // 2, 2 * LANES), jnp.bfloat16),
            pltpu.VMEM((SPANS, PPG, 2, FLOC, LANES), jnp.bfloat16),
            pltpu.SemaphoreType.DMA((2,)),
            pltpu.SemaphoreType.DMA((SPANS,)),
            pltpu.SemaphoreType.DMA((SPANS,)),
        ],
        input_output_aliases={} if late else {7: 0},
        compiler_params=pltpu.CompilerParams(vmem_limit_bytes=VMEM),
        cost_estimate=pl.CostEstimate(flops=2 * 512 * 1024 * 2048, bytes_accessed=9 << 20, transcendentals=0),
        name="front",
    )(raw, halo, weights, table, cosine, sine, base, prev)


def back_kernel(volt_ref, slot_ref, row_ref, table_ref, out_ref, place_ref, v_ref, vs_ref, beam_ref):
    step = pl.program_id(0)
    wide = 2 * LANES
    for x in range(2):
        v_ref[:, x * LANES : (x + 1) * LANES] = volt_ref[:, 0, 0, x].reshape(FEEDS, LANES)

    @pl.when(step == 0)
    def _():
        slots = slot_ref[...]
        for r in range(FEEDS // NS):
            row = lax.broadcasted_iota(jnp.int32, (NS, FEEDS), 0) + r * NS
            place_ref[r * NS : (r + 1) * NS, :] = jnp.where(row == slots, 1.0, 0.0).astype(jnp.bfloat16)

    for at in range(0, FEEDS, BEAMS):
        placed = jnp.dot(place_ref[at : at + BEAMS, :], v_ref[...], preferred_element_type=jnp.float32)
        vs_ref[at : at + BEAMS, :] = placed.astype(jnp.bfloat16)

    for pol in range(POLS):
        parts = []
        for c in range(EW):
            at = (pol * EW + c) * NS
            both = jnp.dot(row_ref[...], vs_ref[at : at + NS, :], preferred_element_type=jnp.float32)
            cosine, sine = both[:NS], both[NS:]
            parts.append((cosine[:, :LANES] - sine[:, LANES:], cosine[:, LANES:] + sine[:, :LANES]))
        (r0, i0), (r1, i1), (r2, i2), (r3, i3) = parts
        ar, ai, br, bi = r0 + r2, i0 + i2, r0 - r2, i0 - i2
        cr, ci, dr, di = r1 + r3, i1 + i3, r1 - r3, i1 - i3
        formed = [(ar + cr, ai + ci), (br - di, bi + dr), (ar - cr, ai - ci), (br + di, bi - dr)]
        for e in range(EW):
            for x in range(2):
                beam_ref[step, pol, e * NS : (e + 1) * NS, x * LANES : (x + 1) * LANES] = formed[e][x].astype(
                    jnp.bfloat16
                )

    for n in range(4):

        @pl.when(step == n)
        def _(n=n):
            for at in range(0, BEAMS, NS):
                total = None
                for pol in range(POLS):
                    bands = None
                    for j in range(n + 1):
                        tap = (3 - n + j) * wide
                        part = jnp.dot(
                            beam_ref[j, pol, at : at + NS, :],
                            table_ref[tap : tap + wide, :],
                            preferred_element_type=jnp.float32,
                        )
                        bands = part if bands is None else bands + part
                    power = bands * bands
                    total = power if total is None else total + power
                value = (total[:, :LANES] + total[:, LANES:]) * (1.0 / UP)
                out_ref[at // 16 : at // 16 + NS // 16, 0, 0] = value.reshape(NS // 16, 16, LANES).astype(jnp.bfloat16)


def back(volt, slots, rows, table):
    return pl.pallas_call(
        back_kernel,
        grid=(4,),
        in_specs=[
            pl.BlockSpec((PEERS // 2, 1, 1, 2, FLOC, LANES), lambda j: (0, j // 2, j % 2, 0, 0, 0)),
            pl.BlockSpec((1, FEEDS), lambda j: (0, 0)),
            pl.BlockSpec((2 * NS, NS), lambda j: (0, 0)),
            pl.BlockSpec((4 * 2 * LANES, 2 * LANES), lambda j: (0, 0)),
        ],
        out_specs=pl.BlockSpec((BEAMS // 16, 1, 1, 16, LANES), lambda j: (0, j // 2, j % 2, 0, 0)),
        out_shape=jax.ShapeDtypeStruct((BEAMS // 16, 2, 2, 16, LANES), jnp.bfloat16),
        scratch_shapes=[
            pltpu.VMEM((FEEDS, FEEDS), jnp.bfloat16),
            pltpu.VMEM((FEEDS, 2 * LANES), jnp.bfloat16),
            pltpu.VMEM((FEEDS, 2 * LANES), jnp.bfloat16),
            pltpu.VMEM((4, POLS, BEAMS, 2 * LANES), jnp.bfloat16),
        ],
        compiler_params=pltpu.CompilerParams(vmem_limit_bytes=VMEM),
        cost_estimate=pl.CostEstimate(flops=14 << 30, bytes_accessed=6 << 20, transcendentals=0),
        name="back",
    )(volt.reshape(PEERS // 2, 2, 2, 2, FLOC, LANES), slots, rows, table)


def body(raw_samples, delays, grid_slot):
    rim = raw_samples[:, raw_samples.shape[1] - (PTAPS - 1) * NFFT :]
    halo = lax.ppermute(rim, "gy", [(0, 1)])
    steps = jnp.concatenate([2 * jnp.arange(LANES), 256 * (jnp.arange(8) // 2) + jnp.arange(8) % 2]).astype(jnp.int32)
    phases = (delays[:, None] * steps[None, :] % NFFT).astype(jnp.float32) * (2.0 * math.pi / NFFT)
    cosine, sine = jnp.cos(phases), jnp.sin(phases)
    base = jnp.concatenate([cosine[:, LANES:], sine[:, LANES:]], axis=1)
    cosine, sine = cosine[:, :LANES], sine[:, :LANES]
    weights = jnp.asarray(taper(PTAPS, NFFT))
    table = jnp.asarray(dft_table())
    rows = jnp.asarray(row_table())
    me = lax.axis_index(BOTH)
    sub = lax.dynamic_slice_in_dim(jnp.asarray(sub_table()), PPG - me % PPG, PPG, axis=2)
    sub = sub.reshape(UTAPS * 2 * LANES, 2 * LANES)

    volt = front(True, raw_samples, rim, weights, table, cosine, sine, base, rim)
    volt = front(False, raw_samples, halo, weights, table, cosine, sine, base, volt)
    volt = lax.all_to_all(volt, BOTH, 0, 0, tiled=True)
    intens = back(volt, grid_slot.reshape(1, FEEDS), rows, sub).reshape(PEERS, 2, 16, LANES)
    intens = lax.all_to_all(intens, BOTH, 0, 0, tiled=True)
    return jnp.transpose(intens, (2, 1, 0, 3)).reshape(16, 2, CHAN * UP)


def solution(mesh):
    return jax.shard_map(
        body,
        mesh=mesh,
        in_specs=(P("gx", "gy"), P("gx"), P()),
        out_specs=P("gx", "gy", None),
        check_vma=False,
    )
```

profile of v0, /device:TPU:1, one launch (start us, length us, event | category | flops | bytes accessed | tf_op | source)
XLA Modules:
  0.0 137.1 jit_solution(2392467502675293469)
XLA Ops:
  0.0 1.0 slice.15.halo_ref.prev_ref
  1.0 0.0 copy-start
  1.0 4.0 %collective-permute-start = (bf16[32,6144]{1,0:T(8,128)(2,1)S(1)}, bf16[32,6144]{1,0:T(8,128)(2,1)S(1)}, u32[]{:S(2)}, u32[]{:S(2)}) collective-permute-start(bf16[32,6144]{1,0:T(8,128)(2,1)S(1)} %slice.15.halo_ref.prev_ref), channel_id=1, source_target_pairs={{0,1},{2,3},{4,5},{6,7},{8,9},{10,11},{12,13},{14,15},{16,17},{18,... | collective-permute-start | bytes 1179656 | tf_op jit(solution)/shard_map/ppermute | solution.py:271
  5.1 0.9 fusion.3
  5.9 0.6 slice.21.sin_ref
  6.5 0.6 slice.20.cos_ref
  7.1 0.7 pad_maximum_fusion.base_ref
  7.8 0.0 copy-done
  7.8 9.4 %front.2.prev_ref = bf16[128,2,2,32,128]{4,3,2,1,0:T(8,128)(2,1)} custom-call(bf16[32,65536]{1,0:T(8,128)(2,1)} %raw_ref.3, bf16[32,6144]{1,0:T(8,128)(2,1)} %copy-done, f32[4,2048]{1,0:T(4,128)} %constant.80.clone.w_ref, bf16[4,2,1024,256]{3,2,1,0:T(8,128)(2,1)} %constant.81.clone.tab_ref, f32[32,128]{1,0:T(8,128)} %slice.20.cos_ref, ...), custom_call_target="tpu_custom_call" | custom-call | flops 2147483648 | bytes 9437184 | tf_op jit(solution)/shard_map/front/pallas_call | solution.py:168
  17.2 0.0 collective-permute-done.halo_ref
  17.2 0.0 copy-start.1
  17.3 0.7 copy-done.1
  18.0 9.4 %front.3 = bf16[128,2,2,32,128]{4,3,2,1,0:T(8,128)(2,1)} custom-call(bf16[32,65536]{1,0:T(8,128)(2,1)} %raw_ref.3, bf16[32,6144]{1,0:T(8,128)(2,1)} %copy-done.1, f32[4,2048]{1,0:T(4,128)} %constant.80.clone.w_ref, bf16[4,2,1024,256]{3,2,1,0:T(8,128)(2,1)} %constant.81.clone.tab_ref, f32[32,128]{1,0:T(8,128)} %slice.20.cos_ref, ...), custom_call_target="tpu_custom_call", output_to_operand_aliasing={{}: (7, {})} | custom-call | flops 2147483648 | bytes 9437184 | tf_op jit(solution)/shard_map/front/pallas_call | solution.py:168
  27.4 0.0 copy-start.2
  27.4 11.1 %all-to-all-start = ((bf16[128,2,2,32,128]{4,3,2,1,0:T(8,128)(2,1)}), bf16[128,2,2,32,128]{4,3,2,1,0:T(8,128)(2,1)}, u32[]{:S(2)}, u32[]{:S(2)}) async-start(bf16[128,2,2,32,128]{4,3,2,1,0:T(8,128)(2,1)} %front.3), calls=%async_computation | async-start | bytes 8388608 | tf_op jit(solution)/shard_map/all_to_all | solution.py:286
  38.6 0.0 copy-done.2
  38.6 0.2 constant_dynamic-slice_fusion
  38.8 1.0 reshape.19.table_ref
  39.8 51.2 %all-to-all-done = bf16[128,2,2,32,128]{4,3,2,1,0:T(8,128)(2,1)} async-done(((bf16[128,2,2,32,128]{4,3,2,1,0:T(8,128)(2,1)}), bf16[128,2,2,32,128]{4,3,2,1,0:T(8,128)(2,1)}, u32[]{:S(2)}, u32[]{:S(2)}) %all-to-all-start) | async-done | bytes 4194336 | tf_op jit(solution)/shard_map/all_to_all | solution.py:286
  91.0 19.7 %back.1 = bf16[64,2,2,16,128]{4,3,2,1,0:T(8,128)(2,1)} custom-call(bf16[64,2,2,2,32,128]{5,4,3,2,1,0:T(8,128)(2,1)} %bitcast.volt_ref, s32[1,2048]{1,0:T(1,128)} %bitcast.8, bf16[512,256]{1,0:T(8,128)(2,1)} %constant.82.clone.row_ref, bf16[1024,256]{1,0:T(8,128)(2,1)} %reshape.19.table_ref), custom_call_target="tpu_custom_call" | custom-call | flops 15032385536 | bytes 6291456 | tf_op jit(solution)/shard_map/back/pallas_call | solution.py:246
  110.6 25.0 %all_to_all.10 = bf16[128,2,16,128]{3,2,1,0:T(8,128)(2,1)S(1)} all-to-all(bf16[128,2,16,128]{3,2,1,0:T(8,128)(2,1)} %bitcast.7), channel_id=1, replica_groups=mesh['gx'=64,'gy'=2] {'gx','gy'}, dimensions={0} | all-to-all | bytes 2097152 | tf_op jit(solution)/shard_map/all_to_all | solution.py:288
  135.6 0.4 copy.9
  136.0 1.1 reshape.21
  (5 shorter events, 0.0 us)
Async XLA Ops:
  1.0 6.8 %copy-start = (bf16[32,6144]{1,0:T(8,128)(2,1)}, bf16[32,6144]{1,0:T(8,128)(2,1)S(1)}, u32[]{:S(2)}) copy-start(bf16[32,6144]{1,0:T(8,128)(2,1)S(1)} %slice.15.halo_ref.prev_ref) | copy-start | bytes 1179652
  1.0 16.2 %collective-permute-start = (bf16[32,6144]{1,0:T(8,128)(2,1)S(1)}, bf16[32,6144]{1,0:T(8,128)(2,1)S(1)}, u32[]{:S(2)}, u32[]{:S(2)}) collective-permute-start(bf16[32,6144]{1,0:T(8,128)(2,1)S(1)} %slice.15.halo_ref.prev_ref), channel_id=1, source_target_pairs={{0,1},{2,3},{4,5},{6,7},{8,9},{10,11},{12,13},{14,15},{16,17},{18,... | collective-permute-start | bytes 1179656 | tf_op jit(solution)/shard_map/ppermute | solution.py:271
  17.2 0.7 copy-start.1
  27.4 11.2 %copy-start.2 = (bf16[4,2,64,4,256]{4,3,2,1,0:T(4,128)(2,1)S(1)}, bf16[4,2,64,4,256]{4,3,2,1,0:T(4,128)(2,1)}, u32[]{:S(2)}) copy-start(bf16[4,2,64,4,256]{4,3,2,1,0:T(4,128)(2,1)} %constant.83.clone) | copy-start | bytes 3145732
  27.4 63.5 %all-to-all-start = ((bf16[128,2,2,32,128]{4,3,2,1,0:T(8,128)(2,1)}), bf16[128,2,2,32,128]{4,3,2,1,0:T(8,128)(2,1)}, u32[]{:S(2)}, u32[]{:S(2)}) async-start(bf16[128,2,2,32,128]{4,3,2,1,0:T(8,128)(2,1)} %front.3), calls=%async_computation | async-start | bytes 8388608 | tf_op jit(solution)/shard_map/all_to_all | solution.py:286
where the time goes:
time: 138 us; the launch traced here: 137 us
  waiting for transfers between devices  51.2 us (37%)
  Pallas kernels  38.5 us (28%)
  blocking collectives  25 us (18%)
  starting transfers between devices  15.1 us (11%)
  local copies, waits for them, and re-layouts  5.66 us (4%)
  other arithmetic  1.56 us (1%)
    all_to_all x1, waiting for transfers between devices, body(): volt = lax.all_to_all(volt, BOTH, 0, 0, tiled=True)  51.2 us
    all_to_all x1, blocking collectives, body(): intens = lax.all_to_all(intens, BOTH, 0, 0, tiled=True)  25 us
    pallas_call x1, Pallas kernels, back(): pl.pallas_call(back_kernel, grid=(4,), in_specs=[pl.BlockSpec((PEERS // 2...  19.7 us
    pallas_call x2, Pallas kernels, front(): pl.pallas_call(functools.partial(front_kernel, late), in_specs=[there, th...  18.9 us
    all_to_all x1, starting transfers between devices, body(): volt = lax.all_to_all(volt, BOTH, 0, 0, tiled=True)  11.1 us
    ppermute x1, starting transfers between devices, body(): halo = lax.ppermute(rim, 'gy', [(0, 1)])  3.97 us
  transfers between devices with their start and end apart: 2, of which 1 were waited for; matrix products, arithmetic and copies ran while one was open for 3% of the time, Pallas kernels for 7%

commit v1 on v0

--- a/solution.py
+++ b/solution.py
@@ -30,7 +30,8 @@
 FLOC = 32
 HALF = 16
 BOTH = ("gx", "gy")
-VMEM = 56 * 1024 * 1024
+MIB = 1024 * 1024
+SPARE = 16
 
 
 def taper(tap_count, seg_length):
@@ -74,11 +75,21 @@
     return np.concatenate([table, table], axis=2).astype(ml_dtypes.bfloat16)
 
 
-def front_kernel(late, raw_ref, halo_ref, w_ref, tab_ref, cos_ref, sin_ref, base_ref, prev_ref, out_ref, *scratch):
-    del prev_ref
-    ext_ref, x_ref, t_ref, o_ref, raw_sems, tab_sems, out_sems = scratch
+def turns(index):
+    quarter = (index + NFFT // 8) // (NFFT // 4)
+    angle = (index - quarter * (NFFT // 4)).astype(jnp.float32) * (2.0 * math.pi / NFFT)
+    sq = angle * angle
+    sine = angle * (1.0 + sq * (-1.0 / 6 + sq * (1.0 / 120 + sq * (-1.0 / 5040 + sq * (1.0 / 362880)))))
+    cosine = 1.0 + sq * (-1.0 / 2 + sq * (1.0 / 24 + sq * (-1.0 / 720 + sq * (1.0 / 40320 - sq * (1.0 / 3628800)))))
+    odd = quarter % 2 == 1
+    first, second = jnp.where(odd, -sine, cosine), jnp.where(odd, cosine, sine)
+    back = (quarter // 2) % 2 == 1
+    return jnp.where(back, -first, first), jnp.where(back, -second, second)
+
+
+def front_kernel(late, raw_ref, halo_ref, delay_ref, w_ref, tab_ref, out_ref, *scratch):
+    ext_ref, x_ref, t_ref, o_ref, cos_ref, sin_ref, raw_sems, tab_sems, out_sems = scratch
     lead = (PTAPS - 1) * NFFT
-    part = 1 if late else 0
     if late:
         copies = [
             pltpu.make_async_copy(
@@ -93,10 +104,25 @@
             ),
         ]
     tables = [pltpu.make_async_copy(tab_ref.at[s], t_ref.at[s], tab_sems.at[s]) for s in range(SPANS)]
-    for copy in copies + tables:
-        copy.start()
+    for copy in copies:
+        copy.start()
+
+    sub = lax.broadcasted_iota(jnp.int32, (8, LANES), 0)
+    lane = lax.broadcasted_iota(jnp.int32, (8, LANES), 1)
+    for g in range(FLOC // 8):
+        delay = jnp.zeros((8, LANES), jnp.int32)
+        for i in range(8):
+            delay = jnp.where(sub == i, delay_ref[g * 8 + i], delay)
+        for s in range(SPANS):
+            for odd in range(2):
+                cosine, sine = turns((delay * (2 * LANES * s + odd + 2 * lane)) % NFFT)
+                cos_ref[s * 2 + odd, g * 8 : g * 8 + 8, :] = cosine
+                sin_ref[s * 2 + odd, g * 8 : g * 8 + 8, :] = sine
+
     for copy in copies:
         copy.wait()
+    for copy in tables:
+        copy.start()
 
     def tile(step, carry):
         at = pl.multiple_of(step * LANES, LANES)
@@ -133,12 +159,9 @@
         spectra = [jnp.dot(x_ref[odd], t_ref[s, odd], preferred_element_type=jnp.float32) for odd in range(2)]
         for h in range(2):
             rows = slice(h * 16, h * 16 + 16)
-            cl, sl = cos_ref[rows, :], sin_ref[rows, :]
             parts = [[None] * PPG, [None] * PPG]
             for odd in range(2):
-                at = s * 2 + odd
-                ca, sa = base_ref[rows, at : at + 1], base_ref[rows, 8 + at : 9 + at]
-                cosine, sine = ca * cl - sa * sl, sa * cl + ca * sl
+                cosine, sine = cos_ref[s * 2 + odd, rows, :], sin_ref[s * 2 + odd, rows, :]
                 for m in range(HALF):
                     i = m * 2 + odd
                     row = h * 256 + m * 16
@@ -154,55 +177,65 @@
                     held = [jnp.where(bits[t], held[(i + (1 << t)) % PPG], held[i]) for i in range(PPG)]
                 for p in range(PPG):
                     o_ref[s, p, x, rows, :] = held[(PPG - p) % PPG]
-        copy = pltpu.make_async_copy(o_ref.at[s], out_ref.at[pl.ds(s * PPG, PPG), part], out_sems.at[s])
+        copy = pltpu.make_async_copy(o_ref.at[s], out_ref.at[pl.ds(s * PPG, PPG)], out_sems.at[s])
         copy.start()
         outs.append(copy)
     for copy in outs:
         copy.wait()
 
 
-def front(late, raw, halo, weights, table, cosine, sine, base, prev):
+def front(late, raw, halo, delays, weights, table):
     wide = (HALF + PTAPS - 1) * NFFT
-    whole = pl.BlockSpec(memory_space=pltpu.VMEM)
     there = pl.BlockSpec(memory_space=pl.ANY)
     return pl.pallas_call(
         functools.partial(front_kernel, late),
-        in_specs=[there, there, whole, there, whole, whole, whole, there],
+        in_specs=[
+            pl.BlockSpec(memory_space=pltpu.HBM),
+            there,
+            pl.BlockSpec(memory_space=pltpu.SMEM),
+            pl.BlockSpec(memory_space=pltpu.VMEM),
+            pl.BlockSpec(memory_space=pltpu.HBM),
+        ],
         out_specs=there,
-        out_shape=jax.ShapeDtypeStruct((PEERS, 2, 2, FLOC, LANES), jnp.bfloat16),
+        out_shape=jax.ShapeDtypeStruct((PEERS, 2, FLOC, LANES), jnp.bfloat16),
         scratch_shapes=[
             pltpu.VMEM((FLOC, wide), jnp.bfloat16),
             pltpu.VMEM((2, FLOC * HALF, NFFT // 2), jnp.bfloat16),
             pltpu.VMEM((SPANS, 2, NFFT // 2, 2 * LANES), jnp.bfloat16),
             pltpu.VMEM((SPANS, PPG, 2, FLOC, LANES), jnp.bfloat16),
+            pltpu.VMEM((2 * SPANS, FLOC, LANES), jnp.float32),
+            pltpu.VMEM((2 * SPANS, FLOC, LANES), jnp.float32),
             pltpu.SemaphoreType.DMA((2,)),
             pltpu.SemaphoreType.DMA((SPANS,)),
             pltpu.SemaphoreType.DMA((SPANS,)),
         ],
-        input_output_aliases={} if late else {7: 0},
-        compiler_params=pltpu.CompilerParams(vmem_limit_bytes=VMEM),
+        compiler_params=pltpu.CompilerParams(vmem_limit_bytes=(58 if late else 30) * MIB),
         cost_estimate=pl.CostEstimate(flops=2 * 512 * 1024 * 2048, bytes_accessed=9 << 20, transcendentals=0),
-        name="front",
-    )(raw, halo, weights, table, cosine, sine, base, prev)
-
-
-def back_kernel(volt_ref, slot_ref, row_ref, table_ref, out_ref, place_ref, v_ref, vs_ref, beam_ref):
-    step = pl.program_id(0)
-    wide = 2 * LANES
-    for x in range(2):
-        v_ref[:, x * LANES : (x + 1) * LANES] = volt_ref[:, 0, 0, x].reshape(FEEDS, LANES)
-
-    @pl.when(step == 0)
-    def _():
-        slots = slot_ref[...]
-        for r in range(FEEDS // NS):
-            row = lax.broadcasted_iota(jnp.int32, (NS, FEEDS), 0) + r * NS
-            place_ref[r * NS : (r + 1) * NS, :] = jnp.where(row == slots, 1.0, 0.0).astype(jnp.bfloat16)
-
+        name="front_late" if late else "front_early",
+    )(raw, halo, delays, weights, table)
+
+
+def fetch_volts(volt_ref, v_ref, sems):
+    return [
+        pltpu.make_async_copy(
+            volt_ref.at[:, gy, x], v_ref.at[gy, :, :, pl.ds(x * LANES, LANES)], sems.at[gy * 2 + x]
+        )
+        for gy in range(2)
+        for x in range(2)
+    ]
+
+
+def mark_places(slot_ref, place_ref):
+    slots = slot_ref[...]
+    for r in range(FEEDS // NS):
+        row = lax.broadcasted_iota(jnp.int32, (NS, FEEDS), 0) + r * NS
+        place_ref[r * NS : (r + 1) * NS, :] = jnp.where(row == slots, 1.0, 0.0).astype(jnp.bfloat16)
+
+
+def form_beams(volts, row_ref, place_ref, vs_ref, store):
     for at in range(0, FEEDS, BEAMS):
-        placed = jnp.dot(place_ref[at : at + BEAMS, :], v_ref[...], preferred_element_type=jnp.float32)
+        placed = jnp.dot(place_ref[at : at + BEAMS, :], volts, preferred_element_type=jnp.float32)
         vs_ref[at : at + BEAMS, :] = placed.astype(jnp.bfloat16)
-
     for pol in range(POLS):
         parts = []
         for c in range(EW):
@@ -216,75 +249,116 @@
         formed = [(ar + cr, ai + ci), (br - di, bi + dr), (ar - cr, ai - ci), (br + di, bi - dr)]
         for e in range(EW):
             for x in range(2):
-                beam_ref[step, pol, e * NS : (e + 1) * NS, x * LANES : (x + 1) * LANES] = formed[e][x].astype(
-                    jnp.bfloat16
-                )
-
-    for n in range(4):
-
-        @pl.when(step == n)
-        def _(n=n):
+                store(pol, e * NS, x * LANES, formed[e][x].astype(jnp.bfloat16))
+
+
+def late_kernel(volt_ref, slot_ref, row_ref, out_ref, place_ref, v_ref, vs_ref, beam_ref, sems):
+    copies = fetch_volts(volt_ref, v_ref, sems)
+    for copy in copies:
+        copy.start()
+    mark_places(slot_ref, place_ref)
+    outs = []
+    for gy in range(2):
+        copies[gy * 2].wait()
+        copies[gy * 2 + 1].wait()
+
+        def store(pol, row, lane, value, gy=gy):
+            beam_ref[gy, pol, row : row + NS, lane : lane + LANES] = value
+
+        form_beams(v_ref[gy].reshape(FEEDS, 2 * LANES), row_ref, place_ref, vs_ref, store)
+        outs.append(pltpu.make_async_copy(beam_ref.at[gy], out_ref.at[gy], sems.at[4 + gy]))
+        outs[gy].start()
+    for copy in outs:
+        copy.wait()
+
+
+def early_kernel(volt_ref, slot_ref, row_ref, late_ref, table_ref, out_ref, place_ref, v_ref, vs_ref, beam_ref, sems):
+    wide = 2 * LANES
+    copies = fetch_volts(volt_ref, v_ref, sems)
+    for gy in range(2):
+        copies.append(
+            pltpu.make_async_copy(
+                late_ref.at[gy], beam_ref.at[:, :, pl.ds((gy * 2 + 1) * wide, wide)], sems.at[4 + gy]
+            )
+        )
+    for copy in copies:
+        copy.start()
+    mark_places(slot_ref, place_ref)
+    for gy in range(2):
+        copies[gy * 2].wait()
+        copies[gy * 2 + 1].wait()
+
+        def store(pol, row, lane, value, gy=gy):
+            at = gy * 2 * wide + lane
+            beam_ref[pol, row : row + NS, at : at + LANES] = value
+
+        form_beams(v_ref[gy].reshape(FEEDS, wide), row_ref, place_ref, vs_ref, store)
+        copies[4 + gy].wait()
+        for n in range(gy * 2, gy * 2 + 2):
             for at in range(0, BEAMS, NS):
                 total = None
                 for pol in range(POLS):
-                    bands = None
-                    for j in range(n + 1):
-                        tap = (3 - n + j) * wide
-                        part = jnp.dot(
-                            beam_ref[j, pol, at : at + NS, :],
-                            table_ref[tap : tap + wide, :],
-                            preferred_element_type=jnp.float32,
-                        )
-                        bands = part if bands is None else bands + part
+                    bands = jnp.dot(
+                        beam_ref[pol, at : at + NS, : (n + 1) * wide],
+                        table_ref[(3 - n) * wide :, :],
+                        preferred_element_type=jnp.float32,
+                    )
                     power = bands * bands
                     total = power if total is None else total + power
                 value = (total[:, :LANES] + total[:, LANES:]) * (1.0 / UP)
-                out_ref[at // 16 : at // 16 + NS // 16, 0, 0] = value.reshape(NS // 16, 16, LANES).astype(jnp.bfloat16)
-
-
-def back(volt, slots, rows, table):
+                out_ref[at // 16 : at // 16 + NS // 16, gy, n % 2] = value.reshape(NS // 16, 16, LANES).astype(
+                    jnp.bfloat16
+                )
+
+
+def back(volt, slots, rows, *more):
+    whole = pl.BlockSpec(memory_space=pltpu.VMEM)
+    there = pl.BlockSpec(memory_space=pl.ANY)
+    far = pl.BlockSpec(memory_space=pltpu.HBM)
+    scratch = [
+        pltpu.VMEM((FEEDS, FEEDS), jnp.bfloat16),
+        pltpu.VMEM((2, PEERS // 2, FLOC, 2 * LANES), jnp.bfloat16),
+        pltpu.VMEM((FEEDS, 2 * LANES), jnp.bfloat16),
+    ]
+    if more:
+        kernel, specs, name = early_kernel, [there, whole, whole, far, whole], "back_early"
+        shape, out = (BEAMS // 16, 2, 2, 16, LANES), whole
+        scratch += [pltpu.VMEM((POLS, BEAMS, 4 * 2 * LANES), jnp.bfloat16), pltpu.SemaphoreType.DMA((6,))]
+    else:
+        kernel, specs, name = late_kernel, [there, whole, whole], "back_late"
+        shape, out = (SPARE, POLS, BEAMS, 2 * LANES), far
+        scratch += [pltpu.VMEM((2, POLS, BEAMS, 2 * LANES), jnp.bfloat16), pltpu.SemaphoreType.DMA((6,))]
     return pl.pallas_call(
-        back_kernel,
-        grid=(4,),
-        in_specs=[
-            pl.BlockSpec((PEERS // 2, 1, 1, 2, FLOC, LANES), lambda j: (0, j // 2, j % 2, 0, 0, 0)),
-            pl.BlockSpec((1, FEEDS), lambda j: (0, 0)),
-            pl.BlockSpec((2 * NS, NS), lambda j: (0, 0)),
-            pl.BlockSpec((4 * 2 * LANES, 2 * LANES), lambda j: (0, 0)),
-        ],
-        out_specs=pl.BlockSpec((BEAMS // 16, 1, 1, 16, LANES), lambda j: (0, j // 2, j % 2, 0, 0)),
-        out_shape=jax.ShapeDtypeStruct((BEAMS // 16, 2, 2, 16, LANES), jnp.bfloat16),
-        scratch_shapes=[
-            pltpu.VMEM((FEEDS, FEEDS), jnp.bfloat16),
-            pltpu.VMEM((FEEDS, 2 * LANES), jnp.bfloat16),
-            pltpu.VMEM((FEEDS, 2 * LANES), jnp.bfloat16),
-            pltpu.VMEM((4, POLS, BEAMS, 2 * LANES), jnp.bfloat16),
-        ],
-        compiler_params=pltpu.CompilerParams(vmem_limit_bytes=VMEM),
-        cost_estimate=pl.CostEstimate(flops=14 << 30, bytes_accessed=6 << 20, transcendentals=0),
-        name="back",
-    )(volt.reshape(PEERS // 2, 2, 2, 2, FLOC, LANES), slots, rows, table)
+        kernel,
+        in_specs=specs,
+        out_specs=out,
+        out_shape=jax.ShapeDtypeStruct(shape, jnp.bfloat16),
+        scratch_shapes=scratch,
+        compiler_params=pltpu.CompilerParams(vmem_limit_bytes=(48 if more else 40) * MIB),
+        cost_estimate=pl.CostEstimate(flops=6 << 30, bytes_accessed=6 << 20, transcendentals=0),
+        name=name,
+    )(volt.reshape(PEERS // 2, 2, 2, FLOC, LANES), slots, rows, *more)
 
 
 def body(raw_samples, delays, grid_slot):
     rim = raw_samples[:, raw_samples.shape[1] - (PTAPS - 1) * NFFT :]
     halo = lax.ppermute(rim, "gy", [(0, 1)])
-    steps = jnp.concatenate([2 * jnp.arange(LANES), 256 * (jnp.arange(8) // 2) + jnp.arange(8) % 2]).astype(jnp.int32)
-    phases = (delays[:, None] * steps[None, :] % NFFT).astype(jnp.float32) * (2.0 * math.pi / NFFT)
-    cosine, sine = jnp.cos(phases), jnp.sin(phases)
-    base = jnp.concatenate([cosine[:, LANES:], sine[:, LANES:]], axis=1)
-    cosine, sine = cosine[:, :LANES], sine[:, :LANES]
     weights = jnp.asarray(taper(PTAPS, NFFT))
     table = jnp.asarray(dft_table())
     rows = jnp.asarray(row_table())
+    slots = grid_slot.reshape(1, FEEDS)
     me = lax.axis_index(BOTH)
     sub = lax.dynamic_slice_in_dim(jnp.asarray(sub_table()), PPG - me % PPG, PPG, axis=2)
     sub = sub.reshape(UTAPS * 2 * LANES, 2 * LANES)
 
-    volt = front(True, raw_samples, rim, weights, table, cosine, sine, base, rim)
-    volt = front(False, raw_samples, halo, weights, table, cosine, sine, base, volt)
-    volt = lax.all_to_all(volt, BOTH, 0, 0, tiled=True)
-    intens = back(volt, grid_slot.reshape(1, FEEDS), rows, sub).reshape(PEERS, 2, 16, LANES)
+    late = front(True, raw_samples, rim, delays, weights, table)
+    late, halo = lax.optimization_barrier((late, halo))
+    late = lax.all_to_all(late, BOTH, 0, 0, tiled=True)
+    early = front(False, raw_samples, halo, delays, weights, table)
+    early, late = lax.optimization_barrier((early, late))
+    early = lax.all_to_all(early, BOTH, 0, 0, tiled=True)
+    beams = back(late, slots, rows)
+    intens = back(early, slots, rows, beams, sub).reshape(PEERS, 2, 16, LANES)
     intens = lax.all_to_all(intens, BOTH, 0, 0, tiled=True)
     return jnp.transpose(intens, (2, 1, 0, 3)).reshape(16, 2, CHAN * UP)
 

time: 138 us -> 127 us (0.920)
  waiting for transfers between devices: 51.2 us -> 39.2 us
  starting transfers between devices: 15.1 us -> 21.3 us
  Pallas kernels: 38.5 us -> 34 us
  local copies, waits for them, and re-layouts: 5.66 us -> 8.34 us
  blocking collectives: 25 us -> 23.1 us
  other arithmetic: 1.56 us -> 0 us
    all_to_all x1 -> x2, waiting for transfers between devices: 51.2 us -> 39.2 us  [the longest x1 20.7 us: body(): early = lax.all_to_all(early, BOTH, 0, 0, tiled=True)]
    all_to_all x1 -> x2, starting transfers between devices: 11.1 us -> 17.4 us  [the longest x1 11.5 us: body(): late = lax.all_to_all(late, BOTH, 0, 0, tiled=True)]
    pallas_call x3 -> x4, Pallas kernels: 38.5 us -> 34 us  [the longest x2 18.1 us: back(): pl.pallas_call(kernel, in_specs=specs, out_specs=out, out_shape=jax.Shape...]
    unnamed x6 -> x14, local copies, waits for them, and re-layouts: 0.75 us -> 4.4 us
    all_to_all x1, blocking collectives: 25 us -> 23.1 us  [body(): intens = lax.all_to_all(intens, BOTH, 0, 0, tiled=True)]
  transfers between devices with their start and end apart: 2 -> 3, of which waited for: 1 -> 2; matrix products, arithmetic and copies ran while one was open for 3% -> 1% of each run, Pallas kernels for 7% -> 19%
where the time goes in v1:
time: 127 us; the launch traced here: 126 us
  waiting for transfers between devices  39.2 us (31%)
  Pallas kernels  34 us (27%)
  blocking collectives  23.1 us (18%)
  starting transfers between devices  21.3 us (17%)
  local copies, waits for them, and re-layouts  8.34 us (7%)
    all_to_all x1, blocking collectives, body(): intens = lax.all_to_all(intens, BOTH, 0, 0, tiled=True)  23.1 us
    all_to_all x1, waiting for transfers between devices, body(): early = lax.all_to_all(early, BOTH, 0, 0, tiled=True)  20.7 us
    all_to_all x1, waiting for transfers between devices, body(): late = lax.all_to_all(late, BOTH, 0, 0, tiled=True)  18.5 us
    pallas_call x2, Pallas kernels, back(): pl.pallas_call(kernel, in_specs=specs, out_specs=out, out_shape=jax.Shape...  18.1 us
    pallas_call x2, Pallas kernels, front(): pl.pallas_call(functools.partial(front_kernel, late), in_specs=[pl.BlockS...  15.9 us
    all_to_all x1, starting transfers between devices, body(): late = lax.all_to_all(late, BOTH, 0, 0, tiled=True)  11.5 us
    all_to_all x1, starting transfers between devices, body(): early = lax.all_to_all(early, BOTH, 0, 0, tiled=True)  5.84 us
    unnamed x14, local copies, waits for them, and re-layouts  4.4 us
  transfers between devices with their start and end apart: 3, of which 2 were waited for; matrix products, arithmetic and copies ran while one was open for 1% of the time, Pallas kernels for 19%

profile of v1, /device:TPU:1, one launch (start us, length us, event | category | flops | bytes accessed | tf_op | source)
XLA Modules:
  0.0 126.1 jit_solution(394412714005294686)
XLA Ops:
  0.0 1.0 slice.3.halo_ref
  1.0 0.0 copy-start.6
  1.0 4.0 %collective-permute-start = (bf16[32,6144]{1,0:T(8,128)(2,1)S(1)}, bf16[32,6144]{1,0:T(8,128)(2,1)S(1)}, u32[]{:S(2)}, u32[]{:S(2)}) collective-permute-start(bf16[32,6144]{1,0:T(8,128)(2,1)S(1)} %slice.3.halo_ref), channel_id=1, source_target_pairs={{0,1},{2,3},{4,5},{6,7},{8,9},{10,11},{12,13},{14,15},{16,17},{18,... | collective-permute-start | bytes 1179656 | tf_op jit(solution)/shard_map/ppermute | solution.py:345
  5.0 0.0 copy-done.6
  5.0 8.4 %front_late.1 = bf16[128,2,32,128]{3,2,1,0:T(8,128)(2,1)} custom-call(bf16[32,65536]{1,0:T(8,128)(2,1)} %raw_ref.3, bf16[32,6144]{1,0:T(8,128)(2,1)} %copy-done.6, s32[32]{0:T(128)} %delay_ref.3, f32[4,2048]{1,0:T(4,128)} %constant.35.clone.w_ref, bf16[4,2,1024,256]{3,2,1,0:T(8,128)(2,1)} %constant.36.clone.tab_ref), custom_call_target="tpu_custom_call" | custom-call | flops 2147483648 | bytes 9437184 | tf_op jit(solution)/shard_map/front_late/pallas_call | solution.py:190
  13.5 0.0 copy-start.2
  13.5 0.0 copy-start.3
  13.5 0.0 collective-permute-done.halo_ref
  13.5 11.5 %all-to-all-start = ((bf16[128,2,32,128]{3,2,1,0:T(8,128)(2,1)}), bf16[128,2,32,128]{3,2,1,0:T(8,128)(2,1)S(1)}, u32[]{:S(2)}, u32[]{:S(2)}) async-start(bf16[128,2,32,128]{3,2,1,0:T(8,128)(2,1)} %front_late.1), calls=%async_computation | async-start | bytes 4194304 | tf_op jit(solution)/shard_map/all_to_all | solution.py:356
  25.0 0.0 copy-done.2
  25.0 0.0 copy-done.3
  25.0 0.0 copy-start
  25.1 2.2 %copy-done = bf16[32,65536]{1,0:T(8,128)(2,1)S(1)} copy-done((bf16[32,65536]{1,0:T(8,128)(2,1)S(1)}, bf16[32,65536]{1,0:T(8,128)(2,1)}, u32[]{:S(2)}) %copy-start) | copy-done | bytes 4194328
  27.2 0.0 copy-start.1
  27.2 2.2 %copy-done.1 = bf16[4,2,1024,256]{3,2,1,0:T(8,128)(2,1)S(1)} copy-done((bf16[4,2,1024,256]{3,2,1,0:T(8,128)(2,1)S(1)}, bf16[4,2,1024,256]{3,2,1,0:T(8,128)(2,1)}, u32[]{:S(2)}) %copy-start.1) | copy-done | bytes 4194328
  29.4 7.4 %front_early.1 = bf16[128,2,32,128]{3,2,1,0:T(8,128)(2,1)} custom-call(bf16[32,65536]{1,0:T(8,128)(2,1)S(1)} %copy-done, bf16[32,6144]{1,0:T(8,128)(2,1)S(1)} %collective-permute-done.halo_ref, s32[32]{0:T(128)S(1)} %copy-done.3, f32[4,2048]{1,0:T(4,128)S(1)} %copy-done.2, bf16[4,2,1024,256]{3,2,1,0:T(8,128)(2,1)S(1)} %copy-done.1), custom_call_target="tpu_custom_call" | custom-call | flops 2147483648 | bytes 9437184 | tf_op jit(solution)/shard_map/front_early/pallas_call | solution.py:190
  36.9 18.5 %all-to-all-done = bf16[128,2,32,128]{3,2,1,0:T(8,128)(2,1)S(1)} async-done(((bf16[128,2,32,128]{3,2,1,0:T(8,128)(2,1)}), bf16[128,2,32,128]{3,2,1,0:T(8,128)(2,1)S(1)}, u32[]{:S(2)}, u32[]{:S(2)}) %all-to-all-start) | async-done | bytes 2097184 | tf_op jit(solution)/shard_map/all_to_all | solution.py:356
  55.3 5.8 %all-to-all-start.1 = ((bf16[128,2,32,128]{3,2,1,0:T(8,128)(2,1)}), bf16[128,2,32,128]{3,2,1,0:T(8,128)(2,1)}, u32[]{:S(2)}, u32[]{:S(2)}) async-start(bf16[128,2,32,128]{3,2,1,0:T(8,128)(2,1)} %front_early.1), calls=%async_computation.1 | async-start | bytes 4194304 | tf_op jit(solution)/shard_map/all_to_all | solution.py:359
  61.2 0.0 copy-start.4
  61.2 0.0 copy-start.5
  61.2 1.3 %constant_dynamic-slice_fusion = bf16[4,2,32,4,256]{4,3,2,1,0:T(4,128)(2,1)S(1)} fusion(bf16[4,2,64,4,256]{4,3,2,1,0:T(4,128)(2,1)} %constant.38.clone, s32[]{:T(128)S(6)} %select_n.11), kind=kLoop, calls=%fused_computation | loop fusion | bytes 1048580 | tf_op jit(solution)/shard_map/dynamic_slice | solution.py:351
  62.5 0.1 reshape.21.table_ref
  62.6 0.0 copy-done.4
  62.6 0.0 copy-done.5
  62.6 7.7 %back_late.1.late_ref = bf16[16,2,1024,256]{3,2,1,0:T(8,128)(2,1)} custom-call(bf16[64,2,2,32,128]{4,3,2,1,0:T(8,128)(2,1)S(1)} %bitcast.7, s32[1,2048]{1,0:T(1,128)S(1)} %bitcast.9, bf16[512,256]{1,0:T(8,128)(2,1)S(1)} %copy-done.5), custom_call_target="tpu_custom_call" | custom-call | flops 6442450944 | bytes 6291456 | tf_op jit(solution)/shard_map/back_late/pallas_call | solution.py:331
  70.3 20.7 %all-to-all-done.1 = bf16[128,2,32,128]{3,2,1,0:T(8,128)(2,1)} async-done(((bf16[128,2,32,128]{3,2,1,0:T(8,128)(2,1)}), bf16[128,2,32,128]{3,2,1,0:T(8,128)(2,1)}, u32[]{:S(2)}, u32[]{:S(2)}) %all-to-all-start.1) | async-done | bytes 2097184 | tf_op jit(solution)/shard_map/all_to_all | solution.py:359
  91.1 10.4 %back_early.1 = bf16[64,2,2,16,128]{4,3,2,1,0:T(8,128)(2,1)S(1)} custom-call(bf16[64,2,2,32,128]{4,3,2,1,0:T(8,128)(2,1)} %bitcast.volt_ref, s32[1,2048]{1,0:T(1,128)S(1)} %bitcast.10, bf16[512,256]{1,0:T(8,128)(2,1)S(1)} %copy-done.5, bf16[16,2,1024,256]{3,2,1,0:T(8,128)(2,1)} %back_late.1.late_ref, bf16[1024,256]{1,0:T(8,128)(2,1)S(1)} %reshape.21.table_ref), custom_call_target="tpu_custom_call" | custom-call | flops 6442450944 | bytes 6291456 | tf_op jit(solution)/shard_map/back_early/pallas_call | solution.py:331
  101.5 23.1 %all_to_all.15 = bf16[128,2,16,128]{3,2,1,0:T(8,128)(2,1)S(1)} all-to-all(bf16[128,2,16,128]{3,2,1,0:T(8,128)(2,1)S(1)} %bitcast.8), channel_id=1, replica_groups=mesh['gx'=64,'gy'=2] {'gx','gy'}, dimensions={0} | all-to-all | bytes 2097152 | tf_op jit(solution)/shard_map/all_to_all | solution.py:362
  124.6 0.4 copy.8
  125.0 1.1 reshape.23
Async XLA Ops:
  1.0 4.0 %copy-start.6 = (bf16[32,6144]{1,0:T(8,128)(2,1)}, bf16[32,6144]{1,0:T(8,128)(2,1)S(1)}, u32[]{:S(2)}) copy-start(bf16[32,6144]{1,0:T(8,128)(2,1)S(1)} %slice.3.halo_ref) | copy-start | bytes 1179652
  1.0 12.5 %collective-permute-start = (bf16[32,6144]{1,0:T(8,128)(2,1)S(1)}, bf16[32,6144]{1,0:T(8,128)(2,1)S(1)}, u32[]{:S(2)}, u32[]{:S(2)}) collective-permute-start(bf16[32,6144]{1,0:T(8,128)(2,1)S(1)} %slice.3.halo_ref), channel_id=1, source_target_pairs={{0,1},{2,3},{4,5},{6,7},{8,9},{10,11},{12,13},{14,15},{16,17},{18,... | collective-permute-start | bytes 1179656 | tf_op jit(solution)/shard_map/ppermute | solution.py:345
  13.5 11.6 %copy-start.2 = (f32[4,2048]{1,0:T(4,128)S(1)}, f32[4,2048]{1,0:T(4,128)}, u32[]{:S(2)}) copy-start(f32[4,2048]{1,0:T(4,128)} %constant.35.clone.w_ref) | copy-start | bytes 98308
  13.5 11.6 %copy-start.3 = (s32[32]{0:T(128)S(1)}, s32[32]{0:T(128)}, u32[]{:S(2)}) copy-start(s32[32]{0:T(128)} %delay_ref.3) | copy-start | bytes 388
  13.5 41.8 %all-to-all-start = ((bf16[128,2,32,128]{3,2,1,0:T(8,128)(2,1)}), bf16[128,2,32,128]{3,2,1,0:T(8,128)(2,1)S(1)}, u32[]{:S(2)}, u32[]{:S(2)}) async-start(bf16[128,2,32,128]{3,2,1,0:T(8,128)(2,1)} %front_late.1), calls=%async_computation | async-start | bytes 4194304 | tf_op jit(solution)/shard_map/all_to_all | solution.py:356
  25.0 2.2 %copy-start = (bf16[32,65536]{1,0:T(8,128)(2,1)S(1)}, bf16[32,65536]{1,0:T(8,128)(2,1)}, u32[]{:S(2)}) copy-start(bf16[32,65536]{1,0:T(8,128)(2,1)} %raw_ref.3) | copy-start | bytes 12582916
  27.2 2.2 %copy-start.1 = (bf16[4,2,1024,256]{3,2,1,0:T(8,128)(2,1)S(1)}, bf16[4,2,1024,256]{3,2,1,0:T(8,128)(2,1)}, u32[]{:S(2)}) copy-start(bf16[4,2,1024,256]{3,2,1,0:T(8,128)(2,1)} %constant.36.clone.tab_ref) | copy-start | bytes 12582916
  55.3 35.7 %all-to-all-start.1 = ((bf16[128,2,32,128]{3,2,1,0:T(8,128)(2,1)}), bf16[128,2,32,128]{3,2,1,0:T(8,128)(2,1)}, u32[]{:S(2)}, u32[]{:S(2)}) async-start(bf16[128,2,32,128]{3,2,1,0:T(8,128)(2,1)} %front_early.1), calls=%async_computation.1 | async-start | bytes 4194304 | tf_op jit(solution)/shard_map/all_to_all | solution.py:359
  61.2 1.5 %copy-start.4 = (s32[2048]{0:T(1024)S(1)}, s32[2048]{0:T(1024)}, u32[]{:S(2)}) copy-start(s32[2048]{0:T(1024)} %param.9) | copy-start | bytes 24580
  61.2 1.4 %copy-start.5 = (bf16[512,256]{1,0:T(8,128)(2,1)S(1)}, bf16[512,256]{1,0:T(8,128)(2,1)}, u32[]{:S(2)}) copy-start(bf16[512,256]{1,0:T(8,128)(2,1)} %constant.37.clone.row_ref) | copy-start | bytes 786436

commit v2 on v1

--- a/solution.py
+++ b/solution.py
@@ -90,21 +90,19 @@
 def front_kernel(late, raw_ref, halo_ref, delay_ref, w_ref, tab_ref, out_ref, *scratch):
     ext_ref, x_ref, t_ref, o_ref, cos_ref, sin_ref, raw_sems, tab_sems, out_sems = scratch
     lead = (PTAPS - 1) * NFFT
-    if late:
-        copies = [
-            pltpu.make_async_copy(
-                raw_ref.at[:, pl.ds(HALF * NFFT - lead, HALF * NFFT + lead)], ext_ref, raw_sems.at[0]
-            )
-        ]
-    else:
-        copies = [
-            pltpu.make_async_copy(halo_ref, ext_ref.at[:, pl.ds(0, lead)], raw_sems.at[0]),
-            pltpu.make_async_copy(
-                raw_ref.at[:, pl.ds(0, HALF * NFFT)], ext_ref.at[:, pl.ds(lead, HALF * NFFT)], raw_sems.at[1]
-            ),
-        ]
+    copies = []
+    for h in range(2):
+        rows = pl.ds(h * 16, 16)
+        if late:
+            pairs = [(raw_ref.at[rows, pl.ds(HALF * NFFT - lead, HALF * NFFT + lead)], ext_ref.at[rows, :])]
+        else:
+            pairs = [
+                (raw_ref.at[rows, pl.ds(0, HALF * NFFT)], ext_ref.at[rows, pl.ds(lead, HALF * NFFT)]),
+                (halo_ref.at[rows, :], ext_ref.at[rows, pl.ds(0, lead)]),
+            ]
+        copies.append([pltpu.make_async_copy(src, dst, raw_sems.at[h, i]) for i, (src, dst) in enumerate(pairs)])
     tables = [pltpu.make_async_copy(tab_ref.at[s], t_ref.at[s], tab_sems.at[s]) for s in range(SPANS)]
-    for copy in copies:
+    for copy in copies[0] + copies[1]:
         copy.start()
 
     sub = lax.broadcasted_iota(jnp.int32, (8, LANES), 0)
@@ -119,37 +117,37 @@
                 cos_ref[s * 2 + odd, g * 8 : g * 8 + 8, :] = cosine
                 sin_ref[s * 2 + odd, g * 8 : g * 8 + 8, :] = sine
 
-    for copy in copies:
-        copy.wait()
-    for copy in tables:
-        copy.start()
-
-    def tile(step, carry):
+    def tile(h, step, carry):
         at = pl.multiple_of(step * LANES, LANES)
         half = NFFT // 2
-        for h in range(2):
-            rows = slice(h * 16, h * 16 + 16)
-            totals = []
-            for side in range(2):
-                weights = [w_ref[p : p + 1, pl.ds(at + side * half, LANES)] for p in range(PTAPS)]
-                frames = [
-                    ext_ref[rows, pl.ds(pl.multiple_of(at + side * half + m * NFFT, LANES), LANES)].astype(jnp.float32)
-                    for m in range(HALF + PTAPS - 1)
-                ]
-                sums = []
-                for m in range(HALF):
-                    total = frames[m] * weights[0]
-                    for p in range(1, PTAPS):
-                        total = total + frames[m + p] * weights[p]
-                    sums.append(total)
-                totals.append(sums)
+        rows = slice(h * 16, h * 16 + 16)
+        totals = []
+        for side in range(2):
+            weights = [w_ref[p : p + 1, pl.ds(at + side * half, LANES)] for p in range(PTAPS)]
+            frames = [
+                ext_ref[rows, pl.ds(pl.multiple_of(at + side * half + m * NFFT, LANES), LANES)].astype(jnp.float32)
+                for m in range(HALF + PTAPS - 1)
+            ]
+            sums = []
             for m in range(HALF):
-                place = pl.ds(h * 256 + m * 16, 16)
-                x_ref[0, place, pl.ds(at, LANES)] = (totals[0][m] + totals[1][m]).astype(jnp.bfloat16)
-                x_ref[1, place, pl.ds(at, LANES)] = (totals[0][m] - totals[1][m]).astype(jnp.bfloat16)
+                total = frames[m] * weights[0]
+                for p in range(1, PTAPS):
+                    total = total + frames[m + p] * weights[p]
+                sums.append(total)
+            totals.append(sums)
+        for m in range(HALF):
+            place = pl.ds(h * 256 + m * 16, 16)
+            x_ref[0, place, pl.ds(at, LANES)] = (totals[0][m] + totals[1][m]).astype(jnp.bfloat16)
+            x_ref[1, place, pl.ds(at, LANES)] = (totals[0][m] - totals[1][m]).astype(jnp.bfloat16)
         return carry
 
-    lax.fori_loop(0, NFFT // 2 // LANES, tile, 0)
+    for h in range(2):
+        for copy in copies[h]:
+            copy.wait()
+        if h == 0:
+            for copy in tables:
+                copy.start()
+        lax.fori_loop(0, NFFT // 2 // LANES, functools.partial(tile, h), 0)
 
     block = lax.broadcasted_iota(jnp.int32, (16, LANES), 1) // (LANES // PPG)
     bits = [(block // (1 << t)) % 2 == 1 for t in range(5)]
@@ -205,7 +203,7 @@
             pltpu.VMEM((SPANS, PPG, 2, FLOC, LANES), jnp.bfloat16),
             pltpu.VMEM((2 * SPANS, FLOC, LANES), jnp.float32),
             pltpu.VMEM((2 * SPANS, FLOC, LANES), jnp.float32),
-            pltpu.SemaphoreType.DMA((2,)),
+            pltpu.SemaphoreType.DMA((2, 2)),
             pltpu.SemaphoreType.DMA((SPANS,)),
             pltpu.SemaphoreType.DMA((SPANS,)),
         ],
@@ -281,12 +279,15 @@
                 late_ref.at[gy], beam_ref.at[:, :, pl.ds((gy * 2 + 1) * wide, wide)], sems.at[4 + gy]
             )
         )
-    for copy in copies:
+    for copy in copies[:2]:
         copy.start()
     mark_places(slot_ref, place_ref)
     for gy in range(2):
         copies[gy * 2].wait()
         copies[gy * 2 + 1].wait()
+        if gy == 0:
+            for copy in copies[2:]:
+                copy.start()
 
         def store(pol, row, lane, value, gy=gy):
             at = gy * 2 * wide + lane

time: 127 us -> 127 us (level)
  no operation moved by 1% of the time
where the time goes in v2:
time: 127 us; the launch traced here: 126 us
  waiting for transfers between devices  38.9 us (31%)
  Pallas kernels  33.9 us (27%)
  blocking collectives  23.1 us (18%)
  starting transfers between devices  21.6 us (17%)
  local copies, waits for them, and re-layouts  8.34 us (7%)
    all_to_all x1, blocking collectives, body(): intens = lax.all_to_all(intens, BOTH, 0, 0, tiled=True)  23.1 us
    all_to_all x1, waiting for transfers between devices, body(): early = lax.all_to_all(early, BOTH, 0, 0, tiled=True)  20.7 us
    all_to_all x1, waiting for transfers between devices, body(): late = lax.all_to_all(late, BOTH, 0, 0, tiled=True)  18.2 us
    pallas_call x2, Pallas kernels, back(): pl.pallas_call(kernel, in_specs=specs, out_specs=out, out_shape=jax.Shape...  18.1 us
    pallas_call x2, Pallas kernels, front(): pl.pallas_call(functools.partial(front_kernel, late), in_specs=[pl.BlockS...  15.8 us
    all_to_all x1, starting transfers between devices, body(): late = lax.all_to_all(late, BOTH, 0, 0, tiled=True)  11.8 us
    all_to_all x1, starting transfers between devices, body(): early = lax.all_to_all(early, BOTH, 0, 0, tiled=True)  5.84 us
    unnamed x14, local copies, waits for them, and re-layouts  4.4 us
  transfers between devices with their start and end apart: 3, of which 2 were waited for; matrix products, arithmetic and copies ran while one was open for 1% of the time, Pallas kernels for 19%

profile of v2, /device:TPU:1, one launch (start us, length us, event | category | flops | bytes accessed | tf_op | source)
XLA Modules:
  0.0 126.1 jit_solution(1002816407097808376)
XLA Ops:
  0.0 1.0 slice.3.halo_ref
  1.0 0.0 copy-start.6
  1.0 4.0 %collective-permute-start = (bf16[32,6144]{1,0:T(8,128)(2,1)S(1)}, bf16[32,6144]{1,0:T(8,128)(2,1)S(1)}, u32[]{:S(2)}, u32[]{:S(2)}) collective-permute-start(bf16[32,6144]{1,0:T(8,128)(2,1)S(1)} %slice.3.halo_ref), channel_id=1, source_target_pairs={{0,1},{2,3},{4,5},{6,7},{8,9},{10,11},{12,13},{14,15},{16,17},{18,... | collective-permute-start | bytes 1179656 | tf_op jit(solution)/shard_map/ppermute | solution.py:346
  5.0 0.0 copy-done.6
  5.0 8.1 %front_late.1 = bf16[128,2,32,128]{3,2,1,0:T(8,128)(2,1)} custom-call(bf16[32,65536]{1,0:T(8,128)(2,1)} %raw_ref.3, bf16[32,6144]{1,0:T(8,128)(2,1)} %copy-done.6, s32[32]{0:T(128)} %delay_ref.3, f32[4,2048]{1,0:T(4,128)} %constant.35.clone.w_ref, bf16[4,2,1024,256]{3,2,1,0:T(8,128)(2,1)} %constant.36.clone.tab_ref), custom_call_target="tpu_custom_call" | custom-call | flops 2147483648 | bytes 9437184 | tf_op jit(solution)/shard_map/front_late/pallas_call | solution.py:188
  13.2 0.0 copy-start.2
  13.2 0.0 copy-start.3
  13.2 0.0 collective-permute-done.halo_ref
  13.2 11.8 %all-to-all-start = ((bf16[128,2,32,128]{3,2,1,0:T(8,128)(2,1)}), bf16[128,2,32,128]{3,2,1,0:T(8,128)(2,1)S(1)}, u32[]{:S(2)}, u32[]{:S(2)}) async-start(bf16[128,2,32,128]{3,2,1,0:T(8,128)(2,1)} %front_late.1), calls=%async_computation | async-start | bytes 4194304 | tf_op jit(solution)/shard_map/all_to_all | solution.py:357
  25.0 0.0 copy-done.2
  25.0 0.0 copy-done.3
  25.0 0.0 copy-start
  25.1 2.2 %copy-done = bf16[32,65536]{1,0:T(8,128)(2,1)S(1)} copy-done((bf16[32,65536]{1,0:T(8,128)(2,1)S(1)}, bf16[32,65536]{1,0:T(8,128)(2,1)}, u32[]{:S(2)}) %copy-start) | copy-done | bytes 4194328
  27.2 0.0 copy-start.1
  27.2 2.2 %copy-done.1 = bf16[4,2,1024,256]{3,2,1,0:T(8,128)(2,1)S(1)} copy-done((bf16[4,2,1024,256]{3,2,1,0:T(8,128)(2,1)S(1)}, bf16[4,2,1024,256]{3,2,1,0:T(8,128)(2,1)}, u32[]{:S(2)}) %copy-start.1) | copy-done | bytes 4194328
  29.4 7.7 %front_early.1 = bf16[128,2,32,128]{3,2,1,0:T(8,128)(2,1)} custom-call(bf16[32,65536]{1,0:T(8,128)(2,1)S(1)} %copy-done, bf16[32,6144]{1,0:T(8,128)(2,1)S(1)} %collective-permute-done.halo_ref, s32[32]{0:T(128)S(1)} %copy-done.3, f32[4,2048]{1,0:T(4,128)S(1)} %copy-done.2, bf16[4,2,1024,256]{3,2,1,0:T(8,128)(2,1)S(1)} %copy-done.1), custom_call_target="tpu_custom_call" | custom-call | flops 2147483648 | bytes 9437184 | tf_op jit(solution)/shard_map/front_early/pallas_call | solution.py:188
  37.1 18.2 %all-to-all-done = bf16[128,2,32,128]{3,2,1,0:T(8,128)(2,1)S(1)} async-done(((bf16[128,2,32,128]{3,2,1,0:T(8,128)(2,1)}), bf16[128,2,32,128]{3,2,1,0:T(8,128)(2,1)S(1)}, u32[]{:S(2)}, u32[]{:S(2)}) %all-to-all-start) | async-done | bytes 2097184 | tf_op jit(solution)/shard_map/all_to_all | solution.py:357
  55.3 5.8 %all-to-all-start.1 = ((bf16[128,2,32,128]{3,2,1,0:T(8,128)(2,1)}), bf16[128,2,32,128]{3,2,1,0:T(8,128)(2,1)}, u32[]{:S(2)}, u32[]{:S(2)}) async-start(bf16[128,2,32,128]{3,2,1,0:T(8,128)(2,1)} %front_early.1), calls=%async_computation.1 | async-start | bytes 4194304 | tf_op jit(solution)/shard_map/all_to_all | solution.py:360
  61.2 0.0 copy-start.4
  61.2 0.0 copy-start.5
  61.2 1.3 %constant_dynamic-slice_fusion = bf16[4,2,32,4,256]{4,3,2,1,0:T(4,128)(2,1)S(1)} fusion(bf16[4,2,64,4,256]{4,3,2,1,0:T(4,128)(2,1)} %constant.38.clone, s32[]{:T(128)S(6)} %select_n.11), kind=kLoop, calls=%fused_computation | loop fusion | bytes 1048580 | tf_op jit(solution)/shard_map/dynamic_slice | solution.py:352
  62.5 0.1 reshape.21.table_ref
  62.6 0.0 copy-done.4
  62.6 0.0 copy-done.5
  62.6 7.7 %back_late.1.late_ref = bf16[16,2,1024,256]{3,2,1,0:T(8,128)(2,1)} custom-call(bf16[64,2,2,32,128]{4,3,2,1,0:T(8,128)(2,1)S(1)} %bitcast.7, s32[1,2048]{1,0:T(1,128)S(1)} %bitcast.9, bf16[512,256]{1,0:T(8,128)(2,1)S(1)} %copy-done.5), custom_call_target="tpu_custom_call" | custom-call | flops 6442450944 | bytes 6291456 | tf_op jit(solution)/shard_map/back_late/pallas_call | solution.py:332
  70.3 20.7 %all-to-all-done.1 = bf16[128,2,32,128]{3,2,1,0:T(8,128)(2,1)} async-done(((bf16[128,2,32,128]{3,2,1,0:T(8,128)(2,1)}), bf16[128,2,32,128]{3,2,1,0:T(8,128)(2,1)}, u32[]{:S(2)}, u32[]{:S(2)}) %all-to-all-start.1) | async-done | bytes 2097184 | tf_op jit(solution)/shard_map/all_to_all | solution.py:360
  91.1 10.4 %back_early.1 = bf16[64,2,2,16,128]{4,3,2,1,0:T(8,128)(2,1)S(1)} custom-call(bf16[64,2,2,32,128]{4,3,2,1,0:T(8,128)(2,1)} %bitcast.volt_ref, s32[1,2048]{1,0:T(1,128)S(1)} %bitcast.10, bf16[512,256]{1,0:T(8,128)(2,1)S(1)} %copy-done.5, bf16[16,2,1024,256]{3,2,1,0:T(8,128)(2,1)} %back_late.1.late_ref, bf16[1024,256]{1,0:T(8,128)(2,1)S(1)} %reshape.21.table_ref), custom_call_target="tpu_custom_call" | custom-call | flops 6442450944 | bytes 6291456 | tf_op jit(solution)/shard_map/back_early/pallas_call | solution.py:332
  101.4 23.1 %all_to_all.15 = bf16[128,2,16,128]{3,2,1,0:T(8,128)(2,1)S(1)} all-to-all(bf16[128,2,16,128]{3,2,1,0:T(8,128)(2,1)S(1)} %bitcast.8), channel_id=1, replica_groups=mesh['gx'=64,'gy'=2] {'gx','gy'}, dimensions={0} | all-to-all | bytes 2097152 | tf_op jit(solution)/shard_map/all_to_all | solution.py:363
  124.6 0.4 copy.8
  125.0 1.1 reshape.23
Async XLA Ops:
  1.0 4.0 %copy-start.6 = (bf16[32,6144]{1,0:T(8,128)(2,1)}, bf16[32,6144]{1,0:T(8,128)(2,1)S(1)}, u32[]{:S(2)}) copy-start(bf16[32,6144]{1,0:T(8,128)(2,1)S(1)} %slice.3.halo_ref) | copy-start | bytes 1179652
  1.0 12.1 %collective-permute-start = (bf16[32,6144]{1,0:T(8,128)(2,1)S(1)}, bf16[32,6144]{1,0:T(8,128)(2,1)S(1)}, u32[]{:S(2)}, u32[]{:S(2)}) collective-permute-start(bf16[32,6144]{1,0:T(8,128)(2,1)S(1)} %slice.3.halo_ref), channel_id=1, source_target_pairs={{0,1},{2,3},{4,5},{6,7},{8,9},{10,11},{12,13},{14,15},{16,17},{18,... | collective-permute-start | bytes 1179656 | tf_op jit(solution)/shard_map/ppermute | solution.py:346
  13.2 11.9 %copy-start.2 = (f32[4,2048]{1,0:T(4,128)S(1)}, f32[4,2048]{1,0:T(4,128)}, u32[]{:S(2)}) copy-start(f32[4,2048]{1,0:T(4,128)} %constant.35.clone.w_ref) | copy-start | bytes 98308
  13.2 11.9 %copy-start.3 = (s32[32]{0:T(128)S(1)}, s32[32]{0:T(128)}, u32[]{:S(2)}) copy-start(s32[32]{0:T(128)} %delay_ref.3) | copy-start | bytes 388
  13.2 42.1 %all-to-all-start = ((bf16[128,2,32,128]{3,2,1,0:T(8,128)(2,1)}), bf16[128,2,32,128]{3,2,1,0:T(8,128)(2,1)S(1)}, u32[]{:S(2)}, u32[]{:S(2)}) async-start(bf16[128,2,32,128]{3,2,1,0:T(8,128)(2,1)} %front_late.1), calls=%async_computation | async-start | bytes 4194304 | tf_op jit(solution)/shard_map/all_to_all | solution.py:357
  25.0 2.2 %copy-start = (bf16[32,65536]{1,0:T(8,128)(2,1)S(1)}, bf16[32,65536]{1,0:T(8,128)(2,1)}, u32[]{:S(2)}) copy-start(bf16[32,65536]{1,0:T(8,128)(2,1)} %raw_ref.3) | copy-start | bytes 12582916
  27.2 2.2 %copy-start.1 = (bf16[4,2,1024,256]{3,2,1,0:T(8,128)(2,1)S(1)}, bf16[4,2,1024,256]{3,2,1,0:T(8,128)(2,1)}, u32[]{:S(2)}) copy-start(bf16[4,2,1024,256]{3,2,1,0:T(8,128)(2,1)} %constant.36.clone.tab_ref) | copy-start | bytes 12582916
  55.3 35.7 %all-to-all-start.1 = ((bf16[128,2,32,128]{3,2,1,0:T(8,128)(2,1)}), bf16[128,2,32,128]{3,2,1,0:T(8,128)(2,1)}, u32[]{:S(2)}, u32[]{:S(2)}) async-start(bf16[128,2,32,128]{3,2,1,0:T(8,128)(2,1)} %front_early.1), calls=%async_computation.1 | async-start | bytes 4194304 | tf_op jit(solution)/shard_map/all_to_all | solution.py:360
  61.2 1.5 %copy-start.4 = (s32[2048]{0:T(1024)S(1)}, s32[2048]{0:T(1024)}, u32[]{:S(2)}) copy-start(s32[2048]{0:T(1024)} %param.9) | copy-start | bytes 24580
  61.2 1.4 %copy-start.5 = (bf16[512,256]{1,0:T(8,128)(2,1)S(1)}, bf16[512,256]{1,0:T(8,128)(2,1)}, u32[]{:S(2)}) copy-start(bf16[512,256]{1,0:T(8,128)(2,1)} %constant.37.clone.row_ref) | copy-start | bytes 786436

commit v3 on v2

--- a/solution.py
+++ b/solution.py
@@ -223,9 +223,9 @@
     ]
 
 
-def mark_places(slot_ref, place_ref):
+def mark_places(slot_ref, place_ref, pol):
     slots = slot_ref[...]
-    for r in range(FEEDS // NS):
+    for r in range(pol * EW, pol * EW + EW):
         row = lax.broadcasted_iota(jnp.int32, (NS, FEEDS), 0) + r * NS
         place_ref[r * NS : (r + 1) * NS, :] = jnp.where(row == slots, 1.0, 0.0).astype(jnp.bfloat16)
 
@@ -254,11 +254,13 @@
     copies = fetch_volts(volt_ref, v_ref, sems)
     for copy in copies:
         copy.start()
-    mark_places(slot_ref, place_ref)
+    mark_places(slot_ref, place_ref, 0)
     outs = []
     for gy in range(2):
         copies[gy * 2].wait()
         copies[gy * 2 + 1].wait()
+        if gy == 0:
+            mark_places(slot_ref, place_ref, 1)
 
         def store(pol, row, lane, value, gy=gy):
             beam_ref[gy, pol, row : row + NS, lane : lane + LANES] = value
@@ -281,13 +283,14 @@
         )
     for copy in copies[:2]:
         copy.start()
-    mark_places(slot_ref, place_ref)
+    mark_places(slot_ref, place_ref, 0)
     for gy in range(2):
         copies[gy * 2].wait()
         copies[gy * 2 + 1].wait()
         if gy == 0:
             for copy in copies[2:]:
                 copy.start()
+            mark_places(slot_ref, place_ref, 1)
 
         def store(pol, row, lane, value, gy=gy):
             at = gy * 2 * wide + lane

time: 127 us -> 127 us (level)
  no operation moved by 1% of the time
where the time goes in v3:
time: 127 us; the launch traced here: 126 us
  waiting for transfers between devices  38.9 us (31%)
  Pallas kernels  33.9 us (27%)
  blocking collectives  23.1 us (18%)
  starting transfers between devices  21.6 us (17%)
  local copies, waits for them, and re-layouts  8.34 us (7%)
    all_to_all x1, blocking collectives, body(): intens = lax.all_to_all(intens, BOTH, 0, 0, tiled=True)  23.1 us
    all_to_all x1, waiting for transfers between devices, body(): early = lax.all_to_all(early, BOTH, 0, 0, tiled=True)  20.8 us
    all_to_all x1, waiting for transfers between devices, body(): late = lax.all_to_all(late, BOTH, 0, 0, tiled=True)  18.2 us
    pallas_call x2, Pallas kernels, back(): pl.pallas_call(kernel, in_specs=specs, out_specs=out, out_shape=jax.Shape...  18.1 us
    pallas_call x2, Pallas kernels, front(): pl.pallas_call(functools.partial(front_kernel, late), in_specs=[pl.BlockS...  15.8 us
    all_to_all x1, starting transfers between devices, body(): late = lax.all_to_all(late, BOTH, 0, 0, tiled=True)  11.8 us
    all_to_all x1, starting transfers between devices, body(): early = lax.all_to_all(early, BOTH, 0, 0, tiled=True)  5.84 us
    unnamed x14, local copies, waits for them, and re-layouts  4.4 us
  transfers between devices with their start and end apart: 3, of which 2 were waited for; matrix products, arithmetic and copies ran while one was open for 1% of the time, Pallas kernels for 19%

profile of v3, /device:TPU:1, one launch (start us, length us, event | category | flops | bytes accessed | tf_op | source)
XLA Modules:
  0.0 126.1 jit_solution(8706109803195582756)
XLA Ops:
  0.0 1.0 slice.3.halo_ref
  1.0 0.0 copy-start.6
  1.0 4.0 %collective-permute-start = (bf16[32,6144]{1,0:T(8,128)(2,1)S(1)}, bf16[32,6144]{1,0:T(8,128)(2,1)S(1)}, u32[]{:S(2)}, u32[]{:S(2)}) collective-permute-start(bf16[32,6144]{1,0:T(8,128)(2,1)S(1)} %slice.3.halo_ref), channel_id=1, source_target_pairs={{0,1},{2,3},{4,5},{6,7},{8,9},{10,11},{12,13},{14,15},{16,17},{18,... | collective-permute-start | bytes 1179656 | tf_op jit(solution)/shard_map/ppermute | solution.py:349
  5.0 0.0 copy-done.6
  5.0 8.1 %front_late.1 = bf16[128,2,32,128]{3,2,1,0:T(8,128)(2,1)} custom-call(bf16[32,65536]{1,0:T(8,128)(2,1)} %raw_ref.3, bf16[32,6144]{1,0:T(8,128)(2,1)} %copy-done.6, s32[32]{0:T(128)} %delay_ref.3, f32[4,2048]{1,0:T(4,128)} %constant.35.clone.w_ref, bf16[4,2,1024,256]{3,2,1,0:T(8,128)(2,1)} %constant.36.clone.tab_ref), custom_call_target="tpu_custom_call" | custom-call | flops 2147483648 | bytes 9437184 | tf_op jit(solution)/shard_map/front_late/pallas_call | solution.py:188
  13.2 0.0 copy-start.2
  13.2 0.0 copy-start.3
  13.2 0.0 collective-permute-done.halo_ref
  13.2 11.8 %all-to-all-start = ((bf16[128,2,32,128]{3,2,1,0:T(8,128)(2,1)}), bf16[128,2,32,128]{3,2,1,0:T(8,128)(2,1)S(1)}, u32[]{:S(2)}, u32[]{:S(2)}) async-start(bf16[128,2,32,128]{3,2,1,0:T(8,128)(2,1)} %front_late.1), calls=%async_computation | async-start | bytes 4194304 | tf_op jit(solution)/shard_map/all_to_all | solution.py:360
  25.0 0.0 copy-done.2
  25.0 0.0 copy-done.3
  25.0 0.0 copy-start
  25.1 2.2 %copy-done = bf16[32,65536]{1,0:T(8,128)(2,1)S(1)} copy-done((bf16[32,65536]{1,0:T(8,128)(2,1)S(1)}, bf16[32,65536]{1,0:T(8,128)(2,1)}, u32[]{:S(2)}) %copy-start) | copy-done | bytes 4194328
  27.2 0.0 copy-start.1
  27.2 2.2 %copy-done.1 = bf16[4,2,1024,256]{3,2,1,0:T(8,128)(2,1)S(1)} copy-done((bf16[4,2,1024,256]{3,2,1,0:T(8,128)(2,1)S(1)}, bf16[4,2,1024,256]{3,2,1,0:T(8,128)(2,1)}, u32[]{:S(2)}) %copy-start.1) | copy-done | bytes 4194328
  29.4 7.7 %front_early.1 = bf16[128,2,32,128]{3,2,1,0:T(8,128)(2,1)} custom-call(bf16[32,65536]{1,0:T(8,128)(2,1)S(1)} %copy-done, bf16[32,6144]{1,0:T(8,128)(2,1)S(1)} %collective-permute-done.halo_ref, s32[32]{0:T(128)S(1)} %copy-done.3, f32[4,2048]{1,0:T(4,128)S(1)} %copy-done.2, bf16[4,2,1024,256]{3,2,1,0:T(8,128)(2,1)S(1)} %copy-done.1), custom_call_target="tpu_custom_call" | custom-call | flops 2147483648 | bytes 9437184 | tf_op jit(solution)/shard_map/front_early/pallas_call | solution.py:188
  37.1 18.2 %all-to-all-done = bf16[128,2,32,128]{3,2,1,0:T(8,128)(2,1)S(1)} async-done(((bf16[128,2,32,128]{3,2,1,0:T(8,128)(2,1)}), bf16[128,2,32,128]{3,2,1,0:T(8,128)(2,1)S(1)}, u32[]{:S(2)}, u32[]{:S(2)}) %all-to-all-start) | async-done | bytes 2097184 | tf_op jit(solution)/shard_map/all_to_all | solution.py:360
  55.3 5.8 %all-to-all-start.1 = ((bf16[128,2,32,128]{3,2,1,0:T(8,128)(2,1)}), bf16[128,2,32,128]{3,2,1,0:T(8,128)(2,1)}, u32[]{:S(2)}, u32[]{:S(2)}) async-start(bf16[128,2,32,128]{3,2,1,0:T(8,128)(2,1)} %front_early.1), calls=%async_computation.1 | async-start | bytes 4194304 | tf_op jit(solution)/shard_map/all_to_all | solution.py:363
  61.2 0.0 copy-start.4
  61.2 0.0 copy-start.5
  61.2 1.3 %constant_dynamic-slice_fusion = bf16[4,2,32,4,256]{4,3,2,1,0:T(4,128)(2,1)S(1)} fusion(bf16[4,2,64,4,256]{4,3,2,1,0:T(4,128)(2,1)} %constant.38.clone, s32[]{:T(128)S(6)} %select_n.11), kind=kLoop, calls=%fused_computation | loop fusion | bytes 1048580 | tf_op jit(solution)/shard_map/dynamic_slice | solution.py:355
  62.5 0.1 reshape.21.table_ref
  62.6 0.0 copy-done.4
  62.6 0.0 copy-done.5
  62.6 7.6 %back_late.1.late_ref = bf16[16,2,1024,256]{3,2,1,0:T(8,128)(2,1)} custom-call(bf16[64,2,2,32,128]{4,3,2,1,0:T(8,128)(2,1)S(1)} %bitcast.7, s32[1,2048]{1,0:T(1,128)S(1)} %bitcast.9, bf16[512,256]{1,0:T(8,128)(2,1)S(1)} %copy-done.5), custom_call_target="tpu_custom_call" | custom-call | flops 6442450944 | bytes 6291456 | tf_op jit(solution)/shard_map/back_late/pallas_call | solution.py:335
  70.3 20.8 %all-to-all-done.1 = bf16[128,2,32,128]{3,2,1,0:T(8,128)(2,1)} async-done(((bf16[128,2,32,128]{3,2,1,0:T(8,128)(2,1)}), bf16[128,2,32,128]{3,2,1,0:T(8,128)(2,1)}, u32[]{:S(2)}, u32[]{:S(2)}) %all-to-all-start.1) | async-done | bytes 2097184 | tf_op jit(solution)/shard_map/all_to_all | solution.py:363
  91.1 10.4 %back_early.1 = bf16[64,2,2,16,128]{4,3,2,1,0:T(8,128)(2,1)S(1)} custom-call(bf16[64,2,2,32,128]{4,3,2,1,0:T(8,128)(2,1)} %bitcast.volt_ref, s32[1,2048]{1,0:T(1,128)S(1)} %bitcast.10, bf16[512,256]{1,0:T(8,128)(2,1)S(1)} %copy-done.5, bf16[16,2,1024,256]{3,2,1,0:T(8,128)(2,1)} %back_late.1.late_ref, bf16[1024,256]{1,0:T(8,128)(2,1)S(1)} %reshape.21.table_ref), custom_call_target="tpu_custom_call" | custom-call | flops 6442450944 | bytes 6291456 | tf_op jit(solution)/shard_map/back_early/pallas_call | solution.py:335
  101.5 23.1 %all_to_all.15 = bf16[128,2,16,128]{3,2,1,0:T(8,128)(2,1)S(1)} all-to-all(bf16[128,2,16,128]{3,2,1,0:T(8,128)(2,1)S(1)} %bitcast.8), channel_id=1, replica_groups=mesh['gx'=64,'gy'=2] {'gx','gy'}, dimensions={0} | all-to-all | bytes 2097152 | tf_op jit(solution)/shard_map/all_to_all | solution.py:366
  124.6 0.4 copy.8
  125.0 1.1 reshape.23
Async XLA Ops:
  1.0 4.0 %copy-start.6 = (bf16[32,6144]{1,0:T(8,128)(2,1)}, bf16[32,6144]{1,0:T(8,128)(2,1)S(1)}, u32[]{:S(2)}) copy-start(bf16[32,6144]{1,0:T(8,128)(2,1)S(1)} %slice.3.halo_ref) | copy-start | bytes 1179652
  1.0 12.1 %collective-permute-start = (bf16[32,6144]{1,0:T(8,128)(2,1)S(1)}, bf16[32,6144]{1,0:T(8,128)(2,1)S(1)}, u32[]{:S(2)}, u32[]{:S(2)}) collective-permute-start(bf16[32,6144]{1,0:T(8,128)(2,1)S(1)} %slice.3.halo_ref), channel_id=1, source_target_pairs={{0,1},{2,3},{4,5},{6,7},{8,9},{10,11},{12,13},{14,15},{16,17},{18,... | collective-permute-start | bytes 1179656 | tf_op jit(solution)/shard_map/ppermute | solution.py:349
  13.2 11.9 %copy-start.2 = (f32[4,2048]{1,0:T(4,128)S(1)}, f32[4,2048]{1,0:T(4,128)}, u32[]{:S(2)}) copy-start(f32[4,2048]{1,0:T(4,128)} %constant.35.clone.w_ref) | copy-start | bytes 98308
  13.2 11.9 %copy-start.3 = (s32[32]{0:T(128)S(1)}, s32[32]{0:T(128)}, u32[]{:S(2)}) copy-start(s32[32]{0:T(128)} %delay_ref.3) | copy-start | bytes 388
  13.2 42.1 %all-to-all-start = ((bf16[128,2,32,128]{3,2,1,0:T(8,128)(2,1)}), bf16[128,2,32,128]{3,2,1,0:T(8,128)(2,1)S(1)}, u32[]{:S(2)}, u32[]{:S(2)}) async-start(bf16[128,2,32,128]{3,2,1,0:T(8,128)(2,1)} %front_late.1), calls=%async_computation | async-start | bytes 4194304 | tf_op jit(solution)/shard_map/all_to_all | solution.py:360
  25.0 2.2 %copy-start = (bf16[32,65536]{1,0:T(8,128)(2,1)S(1)}, bf16[32,65536]{1,0:T(8,128)(2,1)}, u32[]{:S(2)}) copy-start(bf16[32,65536]{1,0:T(8,128)(2,1)} %raw_ref.3) | copy-start | bytes 12582916
  27.2 2.2 %copy-start.1 = (bf16[4,2,1024,256]{3,2,1,0:T(8,128)(2,1)S(1)}, bf16[4,2,1024,256]{3,2,1,0:T(8,128)(2,1)}, u32[]{:S(2)}) copy-start(bf16[4,2,1024,256]{3,2,1,0:T(8,128)(2,1)} %constant.36.clone.tab_ref) | copy-start | bytes 12582916
  55.3 35.7 %all-to-all-start.1 = ((bf16[128,2,32,128]{3,2,1,0:T(8,128)(2,1)}), bf16[128,2,32,128]{3,2,1,0:T(8,128)(2,1)}, u32[]{:S(2)}, u32[]{:S(2)}) async-start(bf16[128,2,32,128]{3,2,1,0:T(8,128)(2,1)} %front_early.1), calls=%async_computation.1 | async-start | bytes 4194304 | tf_op jit(solution)/shard_map/all_to_all | solution.py:363
  61.2 1.5 %copy-start.4 = (s32[2048]{0:T(1024)S(1)}, s32[2048]{0:T(1024)}, u32[]{:S(2)}) copy-start(s32[2048]{0:T(1024)} %param.9) | copy-start | bytes 24580
  61.2 1.4 %copy-start.5 = (bf16[512,256]{1,0:T(8,128)(2,1)S(1)}, bf16[512,256]{1,0:T(8,128)(2,1)}, u32[]{:S(2)}) copy-start(bf16[512,256]{1,0:T(8,128)(2,1)} %constant.37.clone.row_ref) | copy-start | bytes 786436
